TPU v7x, 32 devices: a whole 2x2x4 slice. The times are simulated.
32 devices in a mesh: leaf: 8 (over z, x), sib: 4 (over y, core).
Axes of the slice: x: 2, y: 2, z: 4, core: 2. Of those that a mesh axis runs over, the one named last changes fastest.
Arguments:
- sources: float32 [16384, 128], P(('leaf', 'sib')), may hold values from -8 to 8
- ordering: int32 [16384], P(('leaf', 'sib')), may hold values from 0 to 16383, as said below
- diagonal_inverse: float32 [64, 256, 256], P(('leaf', 'sib')), as said below
- low_rank: float32 [16384, 128], P(('leaf', 'sib'))
- nearby_blocks: bfloat16 [64, 8, 256, 256], P(('leaf', 'sib')), may hold values from -0.125 to 0.125
- near_index: int32 [64, 8], P(('leaf', 'sib')), may hold values from 0 to 63, as said below
Outputs:
- solution: float32 [16384, 128], P(('leaf', 'sib'))
- coefficients: float32 [128, 128], replicated
Inputs may be any that keep to these rules, and one draw needn't show every extreme that they name: `ordering`: each catalog row appears once, and the rows of leaf block i are i * 256 to i * 256 + 255. `near_index`: each entry names a leaf block other than its row's own, at most 2 blocks away from it; the distance 2 occurs. `diagonal_inverse`: each block is symmetric positive definite.
All inputs are finite; a program needn't handle non-finite values.
Results may differ from a plain program's by a relative error of at most 0.0034.
Values may be sent and summed in bfloat16 or wider, within the bound.
A program may use at most 64 MiB of HBM per device.

v0:
```python
import jax
import jax.numpy as jnp
from jax import lax
from jax.sharding import PartitionSpec as P

ITERS = 4


def with_halo(array, sides, width):
    for axis, dim in sides:
        size, length = (lax.axis_size(axis), array.shape[dim])
        up = [(i, (i + 1) % size) for i in range(size - 1)]
        down = [(j, i) for i, j in up]
        last = lax.slice_in_dim(array, length - width, length, axis=dim)
        first = lax.slice_in_dim(array, 0, width, axis=dim)
        before = lax.ppermute(last, axis, up)
        after = lax.ppermute(first, axis, down)
        array = jnp.concatenate([before, array, after], axis=dim)
    return array


def neighbours(rounded, leaf_dev):
    return with_halo(rounded, ((("leaf", "sib"), 0),), leaf_dev)


def totals(projection_partial):
    partner_sum = lax.psum(projection_partial, "sib")
    return lax.psum(partner_sum, "leaf")


def on_device(sources, ordering, diagonal_inverse, low_rank, nearby_blocks, near_index):
    highest_setting = lax.Precision.HIGHEST
    leaf_dev = diagonal_inverse.shape[0]
    leaf_size = diagonal_inverse.shape[1]
    columns = sources.shape[1]
    rank_width = low_rank.shape[1]
    position = lax.axis_index("leaf") * lax.axis_size("sib") + lax.axis_index("sib")
    first_row = position * (leaf_dev * leaf_size)
    local_rows = ordering - first_row
    ordered_rows = sources[local_rows].reshape(leaf_dev, leaf_size, columns)
    block_list = low_rank.reshape(leaf_dev, leaf_size, rank_width)
    lifted_vector = jnp.einsum(
        "zym,zmw->zyw", diagonal_inverse, block_list, precision=highest_setting
    )
    core_partial = jnp.einsum("wju,wjp->up", block_list, lifted_vector, precision=highest_setting)
    scaled_rows = jnp.einsum(
        "zym,zmw->zyw", diagonal_inverse, ordered_rows, precision=highest_setting
    )
    projection_partial = jnp.einsum(
        "wju,wjp->up", block_list, scaled_rows, precision=highest_setting
    )
    core_sum, projected_rows = lax.psum((core_partial, projection_partial), ("leaf", "sib"))
    triangle = jnp.linalg.cholesky(jnp.eye(rank_width, dtype=jnp.float32) + core_sum)

    def finish(current_scaled, projected_now):
        coefficients = jax.scipy.linalg.cho_solve((triangle, True), projected_now)
        result_vector = current_scaled - jnp.einsum(
            "eqb,bd->eqd", lifted_vector, coefficients, precision=highest_setting
        )
        return (result_vector, coefficients)

    iterate, coefficients = finish(scaled_rows, projected_rows)
    first_block = (position - 1) * leaf_dev
    targets = near_index - first_block
    for sweep in range(ITERS):
        rounded = iterate.astype(jnp.bfloat16)
        window = neighbours(rounded, leaf_dev)
        piece_list = window[targets]
        image_vector = jnp.einsum(
            "ptog,ptgh->poh", nearby_blocks, piece_list, preferred_element_type=jnp.float32
        )
        scaled_rows = jnp.einsum(
            "zym,zmw->zyw", diagonal_inverse, ordered_rows - image_vector, precision=highest_setting
        )
        projection_partial = jnp.einsum(
            "wju,wjp->up", block_list, scaled_rows, precision=highest_setting
        )
        projected_rows = totals(projection_partial)
        iterate, coefficients = finish(scaled_rows, projected_rows)
    return (iterate.reshape(leaf_dev * leaf_size, columns), coefficients)


def solution(mesh):
    placed = (
        P(("leaf", "sib"), None),
        P(("leaf", "sib")),
        P(("leaf", "sib"), None, None),
        P(("leaf", "sib"), None),
        P(("leaf", "sib"), None, None, None),
        P(("leaf", "sib"), None),
    )
    return jax.shard_map(
        on_device,
        mesh=mesh,
        in_specs=placed,
        out_specs=(P(("leaf", "sib"), None), P()),
        check_vma=False,
    )
```

profile of v0, /device:TPU:0, one launch (start us, length us, event | category | flops | bytes accessed | tf_op | source)
XLA Modules:
  0.0 665.3 jit_solution(1201294893127932239)
XLA Ops:
  8.1 1.7 fusion.27
  9.8 2.2 convolution_bitcast_fusion.18
  12.1 1.6 gather_fusion
  13.7 1.7 convolution_bitcast_fusion.4
  16.5 125.7 %all-reduce.27.cloned.1.call-done = (f32[128,128]{0,1:T(8,128)}, f32[128,128]{1,0:T(8,128)}) async-done(((f32[128,128]{0,1:T(8,128)}, f32[128,128]{1,0:T(8,128)}), (f32[128,128]{0,1:T(8,128)}, f32[128,128]{1,0:T(8,128)})) %all-reduce.27.cloned.1.call-update) | async-done | bytes 131088 | tf_op jit(solution)/shard_map/psum | solution.py:52
  144.0 11.7 %cholesky.20 = f32[128,128]{1,0:T(8,128)S(1)} custom-call(f32[128,128]{1,0:T(8,128)S(1)} %fusion.26), custom_call_target="Cholesky" | custom-call | tf_op jit(solution)/shard_map/jit(cholesky)/cholesky | solution.py:53
  157.1 9.8 %custom-call.12 = f32[1,128,128]{1,2,0:T(8,128)S(1)} custom-call(f32[1,128,128]{2,1,0:T(8,128)S(1)} %fusion.8), custom_call_target="InvertDiagBlocksLowerTriangular" | custom-call | tf_op jit(solution)/shard_map/jit(_cho_solve)/triangular_solve | solution.py:56
  170.6 3.7 collective-permute-start
  175.5 1.8 pad_maximum_fusion
  177.3 2.6 gather_fusion.1
  179.9 2.0 fusion
  184.4 33.4 %all-reduce.11.cloned.1.call-done = f32[128,128]{0,1:T(8,128)} async-done(((f32[128,128]{0,1:T(8,128)}), f32[128,128]{0,1:T(8,128)}) %all-reduce.11.cloned.1.call-update) | async-done | bytes 65552 | tf_op jit(solution)/shard_map/psum | solution.py:27
  217.8 72.3 %all-reduce.13.cloned.1.call-done = f32[128,128]{0,1:T(8,128)} async-done(((f32[128,128]{0,1:T(8,128)}), f32[128,128]{0,1:T(8,128)}) %all-reduce.13.cloned.1.call-update) | async-done | bytes 65552 | tf_op jit(solution)/shard_map/psum | solution.py:28
  291.4 1.4 fusion.5
  292.8 1.5 collective-permute-start.3
  294.3 2.9 collective-permute-start.2
  298.9 2.6 gather_fusion.2
  301.5 2.0 fusion.1
  305.9 34.4 %all-reduce.15.cloned.1.call-done = f32[128,128]{0,1:T(8,128)} async-done(((f32[128,128]{0,1:T(8,128)}), f32[128,128]{0,1:T(8,128)}) %all-reduce.15.cloned.1.call-update) | async-done | bytes 65552 | tf_op jit(solution)/shard_map/psum | solution.py:27
  340.4 71.7 %all-reduce.17.cloned.1.call-done = f32[128,128]{0,1:T(8,128)} async-done(((f32[128,128]{0,1:T(8,128)}), f32[128,128]{0,1:T(8,128)}) %all-reduce.17.cloned.1.call-update) | async-done | bytes 65552 | tf_op jit(solution)/shard_map/psum | solution.py:28
  413.4 1.4 fusion.6
  416.1 3.0 collective-permute-start.4
  420.9 2.6 gather_fusion.3
  423.5 2.0 fusion.2
  428.0 34.4 %all-reduce.19.cloned.1.call-done = f32[128,128]{0,1:T(8,128)} async-done(((f32[128,128]{0,1:T(8,128)}), f32[128,128]{0,1:T(8,128)}) %all-reduce.19.cloned.1.call-update) | async-done | bytes 65552 | tf_op jit(solution)/shard_map/psum | solution.py:27
  462.5 72.3 %all-reduce.21.cloned.1.call-done = f32[128,128]{0,1:T(8,128)} async-done(((f32[128,128]{0,1:T(8,128)}), f32[128,128]{0,1:T(8,128)}) %all-reduce.21.cloned.1.call-update) | async-done | bytes 65552 | tf_op jit(solution)/shard_map/psum | solution.py:28
  536.1 1.4 fusion.7
  538.7 3.0 collective-permute-start.6
  543.5 2.6 gather_fusion.4
  546.1 2.0 fusion.3
  549.9 34.4 %all-reduce.23.cloned.1.call-done = f32[128,128]{0,1:T(8,128)} async-done(((f32[128,128]{0,1:T(8,128)}), f32[128,128]{0,1:T(8,128)}) %all-reduce.23.cloned.1.call-update) | async-done | bytes 65552 | tf_op jit(solution)/shard_map/psum | solution.py:27
  584.3 71.9 %all-reduce.25.cloned.1.call-done = f32[128,128]{0,1:T(8,128)} async-done(((f32[128,128]{0,1:T(8,128)}), f32[128,128]{0,1:T(8,128)}) %all-reduce.25.cloned.1.call-update) | async-done | bytes 65552 | tf_op jit(solution)/shard_map/psum | solution.py:28
  (84 shorter events, 33.6 us)
Async XLA Ops:
  7.2 172.7 %copy-start = (bf16[2,8,256,256]{3,2,1,0:T(8,128)(2,1)S(1)}, bf16[2,8,256,256]{3,2,1,0:T(8,128)(2,1)}, u32[]{:S(2)}) copy-start(bf16[2,8,256,256]{3,2,1,0:T(8,128)(2,1)} %param.12) | copy-start | bytes 6291460
  7.2 6.5 copy-start.1
  7.2 4.9 copy-start.2
  7.2 135.0 %all-reduce.27.cloned.1.call-start = ((), (), s32[]{:S(2)}) async-start(), calls=%async_computation.8 | async-start | bytes 262144 | tf_op jit(solution)/shard_map/psum | solution.py:52
  9.8 5.6 copy-start.3
  13.7 160.6 %copy-start.8 = (s32[2,8]{1,0:T(2,128)S(1)}, s32[2,8]{1,0:T(2,128)}, u32[]{:S(2)}) copy-start(s32[2,8]{1,0:T(2,128)} %param.13) | copy-start | bytes 196
  16.5 201.3 %all-reduce.11.cloned.1.call-start = ((), (), s32[]{:S(2)}) async-start(), calls=%async_computation | async-start | bytes 131072 | tf_op jit(solution)/shard_map/psum | solution.py:27
  169.3 6.2 collective-permute-start.1
  170.6 4.9 collective-permute-start
  182.6 0.7 copy-start.4
  184.3 105.7 %all-reduce.13.cloned.1.call-start = ((), (), s32[]{:S(2)}) async-start(), calls=%async_computation.1 | async-start | bytes 131072 | tf_op jit(solution)/shard_map/psum | solution.py:28
  217.8 122.6 %all-reduce.15.cloned.1.call-start = ((), (), s32[]{:S(2)}) async-start(), calls=%async_computation.2 | async-start | bytes 131072 | tf_op jit(solution)/shard_map/psum | solution.py:27
  292.8 4.3 collective-permute-start.3
  294.3 3.8 collective-permute-start.2
  304.2 0.7 copy-start.5
  305.9 106.2 %all-reduce.17.cloned.1.call-start = ((), (), s32[]{:S(2)}) async-start(), calls=%async_computation.3 | async-start | bytes 131072 | tf_op jit(solution)/shard_map/psum | solution.py:28
  340.4 122.0 %all-reduce.19.cloned.1.call-start = ((), (), s32[]{:S(2)}) async-start(), calls=%async_computation.4 | async-start | bytes 131072 | tf_op jit(solution)/shard_map/psum | solution.py:27
  414.8 4.3 collective-permute-start.5
  416.1 4.0 collective-permute-start.4
  426.2 0.7 copy-start.6
  427.9 106.8 %all-reduce.21.cloned.1.call-start = ((), (), s32[]{:S(2)}) async-start(), calls=%async_computation.5 | async-start | bytes 131072 | tf_op jit(solution)/shard_map/psum | solution.py:28
  462.4 121.9 %all-reduce.23.cloned.1.call-start = ((), (), s32[]{:S(2)}) async-start(), calls=%async_computation.6 | async-start | bytes 131072 | tf_op jit(solution)/shard_map/psum | solution.py:27
  537.4 4.3 collective-permute-start.7
  538.7 4.0 collective-permute-start.6
  549.8 106.4 %all-reduce.25.cloned.1.call-start = ((), (), s32[]{:S(2)}) async-start(), calls=%async_computation.7 | async-start | bytes 131072 | tf_op jit(solution)/shard_map/psum | solution.py:28
  657.5 1.3 copy-start.7
Sparse Core Ops, SparseCore 0:
  16.6 125.5 all-reduce.26
  184.4 33.2 all-reduce.10
  221.5 68.4 all-reduce.12
  306.0 34.2 all-reduce.14
  343.6 68.4 all-reduce.16
  428.1 34.2 all-reduce.18
  466.2 68.4 all-reduce.20
  550.0 34.2 all-reduce.22
  587.7 68.4 all-reduce.24
where the time goes:
time: 667 us; the launch traced here: 665 us
  waiting for transfers between devices  553 us (83%)
  matrix products  33.6 us (5%)
  other arithmetic  29.7 us (4%)
  starting transfers between devices  18.3 us (3%)
  local copies, waits for them, and re-layouts  16.2 us (2%)
  between operations  14.3 us (2%)
    psum x4, waiting for transfers between devices, totals(): return lax.psum(partner_sum, 'leaf')  288 us
    psum x4, waiting for transfers between devices, totals(): partner_sum = lax.psum(projection_partial, 'sib')  137 us
    psum x1, waiting for transfers between devices, on_device(): lax.psum((core_partial, projection_partial), ('leaf', 'sib'))  126 us
  transfers between devices with their start and end apart: 17, of which 12 were waited for; matrix products, arithmetic and copies ran while one was open for 0% of the time, Pallas kernels for 0%

commit v1 on v0

v1 whole, which is shorter than its diff:
```python
import functools

import jax
import jax.numpy as jnp
from jax import lax
from jax.experimental import pallas as pl
from jax.experimental.pallas import tpu as pltpu
from jax.sharding import PartitionSpec as P

ITERS = 4
MESH = pl.DeviceIdType.MESH
HIGH = lax.Precision.HIGHEST
SUMS = (2, ITERS - 1) + (1,) * ITERS
PIVOTS = 8


def mm(a, b):
    return jnp.dot(a, b, precision=HIGH, preferred_element_type=jnp.float32)


def mm_t(a, b):
    return lax.dot_general(
        a, b, (((0,), (0,)), ((), ())), precision=HIGH, preferred_element_type=jnp.float32
    )


def invert(work):
    size = work.shape[0]
    lane = lax.broadcasted_iota(jnp.int32, (PIVOTS, size), 1)
    sub = lax.broadcasted_iota(jnp.int32, (PIVOTS, size), 0)
    wide = lax.broadcasted_iota(jnp.int32, (size, size), 1)
    for off in range(0, size, PIVOTS):
        panel = work[off : off + PIVOTS, :]
        left = jnp.where(lane < off, -panel, panel)
        for j in range(PIVOTS):
            c = off + j
            inv = 1.0 / panel[j : j + 1, c : c + 1]
            row = jnp.where(lane == c, inv, panel[j : j + 1, :] * inv)
            rest = jnp.where(lane == c, 0.0, panel) - panel[:, c : c + 1] * row
            panel = jnp.where(sub == j, row, rest)
        inside = (wide >= off) & (wide < off + PIVOTS)
        work[...] = jnp.where(inside, 0.0, work[...]) - mm_t(left, panel)
        work[off : off + PIVOTS, :] = panel


class Sum:
    def __init__(self, me, sizes, refs):
        self.leaf, self.sib = me
        self.n_leaf, self.n_sib = sizes
        self.src, self.r1, self.r2, self.r3, *self.sems = refs
        self.chunk = self.r1.shape[1]
        self.open = []

    def copy(self, src, dst, phase, o, target):
        send, recv = self.sems[2 * phase], self.sems[2 * phase + 1]
        c = pltpu.make_async_remote_copy(
            src_ref=src, dst_ref=dst, send_sem=send.at[o], recv_sem=recv.at[o],
            device_id=target, device_id_type=MESH,
        )
        c.start()
        self.open.append(c)
        return c

    def first(self):
        self.now = []
        for o in range(1, self.n_sib):
            to = lax.rem(self.sib + o, self.n_sib)
            rows = pl.ds(pl.multiple_of(to * self.chunk, 8), self.chunk)
            self.now.append(self.copy(self.src.at[rows], self.r1.at[o], 0, o, (self.leaf, to)))

    def second(self):
        rows = pl.ds(pl.multiple_of(self.sib * self.chunk, 8), self.chunk)
        total = self.src[rows, :]
        for o, c in enumerate(self.now, 1):
            c.wait_recv()
            total += self.r1[o]
        mine = self.r2.at[self.leaf]
        self.r2[self.leaf] = total
        self.now = []
        for o in range(1, self.n_leaf):
            to = lax.rem(self.leaf + o, self.n_leaf)
            self.now.append(self.copy(mine, mine, 1, o, (to, self.sib)))

    def third(self):
        for c in self.now:
            c.wait_recv()
        total = self.r2[0]
        for o in range(1, self.n_leaf):
            total += self.r2[o]
        mine = self.r3.at[self.sib]
        self.r3[self.sib] = total
        self.now = []
        for o in range(1, self.n_sib):
            to = lax.rem(self.sib + o, self.n_sib)
            self.now.append(self.copy(mine, mine, 2, o, (self.leaf, to)))

    def result(self):
        for c in self.now:
            c.wait_recv()
        return jnp.concatenate([self.r3[o] for o in range(self.n_sib)], axis=0)


def kernel(
    sizes, near, order, src, diag, low, nearby, sol, coef, *scratch
):
    n_leaf, n_sib = sizes
    leaf, sib = lax.axis_index("leaf"), lax.axis_index("sib")
    pos = leaf * n_sib + sib
    last = n_leaf * n_sib - 1
    leaf_dev, leaf_size = diag.shape[0], diag.shape[1]
    rank = low.shape[1]
    blocks = [slice(i * leaf_size, (i + 1) * leaf_size) for i in range(leaf_dev)]
    windows, scratch = scratch[: 2 * ITERS - 1], scratch[2 * ITERS - 1 :]
    h_send, h_recv, lifted, lifted_t, powers, x_first, work = scratch[:7]
    scratch = scratch[7:]
    sums = [Sum((leaf, sib), sizes, scratch[10 * i : 10 * i + 10]) for i in range(len(SUMS))]

    def place(p):
        return (p // n_sib, lax.rem(p, n_sib))

    right, left = place(jnp.minimum(pos + 1, last)), place(jnp.maximum(pos - 1, 0))
    has_right, has_left = pos < last, pos > 0

    barrier = pltpu.get_barrier_semaphore()
    for o in range(1, n_sib):
        pl.semaphore_signal(
            barrier, inc=1, device_id=(leaf, lax.rem(sib + o, n_sib)), device_id_type=MESH
        )
    for o in range(1, n_leaf):
        pl.semaphore_signal(
            barrier, inc=1, device_id=(lax.rem(leaf + o, n_leaf), sib), device_id_type=MESH
        )

    @pl.when(has_right)
    def _():
        pl.semaphore_signal(barrier, inc=1, device_id=right, device_id_type=MESH)

    @pl.when(has_left)
    def _():
        pl.semaphore_signal(barrier, inc=1, device_id=left, device_id_type=MESH)

    def halo(k):
        own = windows[k].at[leaf_dev : 2 * leaf_dev]
        up = pltpu.make_async_remote_copy(
            src_ref=own, dst_ref=windows[k].at[0:leaf_dev],
            send_sem=h_send.at[k, 0], recv_sem=h_recv.at[k, 0],
            device_id=right, device_id_type=MESH,
        )
        down = pltpu.make_async_remote_copy(
            src_ref=own, dst_ref=windows[k].at[2 * leaf_dev : 3 * leaf_dev],
            send_sem=h_send.at[k, 1], recv_sem=h_recv.at[k, 1],
            device_id=left, device_id_type=MESH,
        )
        return up, down

    def send_halo(k, values):
        for i in range(leaf_dev):
            windows[k][leaf_dev + i] = values[i].astype(jnp.bfloat16)
        up, down = halo(k)
        pl.when(has_right)(lambda: up.start())
        pl.when(has_left)(lambda: down.start())

    def wait_halo(k):
        up, down = halo(k)
        pl.when(has_left)(lambda: up.wait_recv())
        pl.when(has_right)(lambda: down.wait_recv())

    def near_apply(k):
        out = []
        for i in range(leaf_dev):
            total = None
            for m in range(near.shape[1]):
                t = jnp.clip(near[i, m] - (pos - 1) * leaf_dev, 0, 3 * leaf_dev - 1)
                part = jnp.dot(nearby[i, m], windows[k][t], preferred_element_type=jnp.float32)
                total = part if total is None else total + part
            out.append(total)
        return out

    def project(values):
        return sum(mm(lifted_t[:, blocks[i]], values[i]) for i in range(leaf_dev))

    core = jnp.zeros((rank, rank), jnp.float32)
    first = jnp.zeros((rank, src.shape[1]), jnp.float32)
    row_ids = lax.broadcasted_iota(jnp.int32, (leaf_size, leaf_size), 0)
    scaled = []
    for i, rows in enumerate(blocks):
        block = low[rows, :]
        up = mm(diag[i], block)
        lifted[rows, :] = up
        up_t = up.T
        lifted_t[:, rows] = up_t
        core += mm(up_t, block)
        local = order[i] - (pos * leaf_dev + i) * leaf_size
        pick = (row_ids == local).astype(jnp.float32)
        ordered = mm_t(pick, src[rows, :])
        scaled.append(mm(diag[i], ordered))
        first += mm(up_t, ordered)
    sums[0].src[0:rank, :] = core
    sums[0].src[rank:, :] = first

    sides = 1 - pos // last + (pos + last - 1) // last
    pl.semaphore_wait(barrier, n_sib + n_leaf - 2 + sides)

    sums[0].first()
    send_halo(0, [lifted[rows, :] for rows in blocks])
    sums[0].second()

    def power(j):
        wait_halo(j)
        image = near_apply(j)
        value = [-mm(diag[i], image[i]) for i in range(leaf_dev)]
        if j + 1 < ITERS - 1:
            send_halo(j + 1, value)
        for i, rows in enumerate(blocks):
            powers[j, rows, :] = value[i]
        sums[1].src[j * rank : (j + 1) * rank, :] = project(image)

    power(0)
    sums[0].third()
    power(1)
    both = sums[0].result()
    eye = lax.broadcasted_iota(jnp.int32, (rank, rank), 0) == lax.broadcasted_iota(
        jnp.int32, (rank, rank), 1
    )
    work[...] = both[:rank] + jnp.where(eye, 1.0, 0.0)
    invert(work)
    c_first = mm(work[...], both[rank:])
    coef[...] = c_first
    now = []
    for i, rows in enumerate(blocks):
        value = scaled[i] - mm(lifted[rows, :], c_first)
        x_first[rows, :] = value
        now.append(value)
    base = ITERS - 1
    send_halo(base, now)
    power(2)
    sums[1].first()
    for k in range(ITERS):
        wait_halo(base + k)
        image = near_apply(base + k)
        now = [x_first[rows, :] - mm(diag[i], image[i]) for i, rows in enumerate(blocks)]
        if k + 1 < ITERS:
            send_halo(base + k + 1, now)
        sums[2 + k].src[...] = project(image)
        sums[2 + k].first()
        if k == 0:
            sums[1].second()
        if k == 1:
            sums[1].third()
        if k >= 1:
            sums[1 + k].second()
        if k >= 2:
            sums[k].third()

    moments = sums[1].result()
    moment = [moments[j * rank : (j + 1) * rank] for j in range(ITERS - 1)]
    deltas = [None]

    def solve(k):
        total = -sums[1 + k].result()
        for j in range(k - 1):
            total += mm(moment[j], deltas[k - 1 - j])
        deltas.append(mm(work[...], total))

    solve(1)
    sums[5].second()
    sums[4].third()
    solve(2)
    solve(3)
    sums[5].third()

    def correct(i, j):
        basis = lifted[blocks[i], :] if j == 0 else powers[j - 1, blocks[i], :]
        return mm(basis, deltas[ITERS - j])

    now = [now[i] - sum(correct(i, j) for j in range(1, ITERS)) for i in range(leaf_dev)]
    solve(4)
    for i, rows in enumerate(blocks):
        sol[rows, :] = now[i] - correct(i, 0)
    coef[...] += deltas[ITERS]

    for s in sums:
        for c in s.open:
            c.wait_send()
    for k in range(2 * ITERS - 1):
        up, down = halo(k)
        pl.when(has_right)(lambda up=up: up.wait_send())
        pl.when(has_left)(lambda down=down: down.wait_send())


def on_device(sources, ordering, diagonal_inverse, low_rank, nearby_blocks, near_index):
    n_leaf, n_sib = lax.axis_size("leaf"), lax.axis_size("sib")
    leaf_dev, leaf_size = diagonal_inverse.shape[:2]
    rows, columns = sources.shape
    rank = low_rank.shape[1]
    f32 = jnp.float32
    scratch = [
        pltpu.VMEM((3 * leaf_dev, leaf_size, columns), jnp.bfloat16) for _ in range(2 * ITERS - 1)
    ]
    scratch += [
        pltpu.SemaphoreType.DMA((2 * ITERS - 1, 2)),
        pltpu.SemaphoreType.DMA((2 * ITERS - 1, 2)),
        pltpu.VMEM((rows, rank), f32),
        pltpu.VMEM((rank, rows), f32),
        pltpu.VMEM((ITERS - 1, rows, rank), f32),
        pltpu.VMEM((rows, columns), f32),
        pltpu.VMEM((rank, rank), f32),
    ]
    for count in SUMS:
        chunk = count * rank // n_sib
        scratch += [
            pltpu.VMEM((count * rank, columns), f32),
            pltpu.VMEM((n_sib, chunk, columns), f32),
            pltpu.VMEM((n_leaf, chunk, columns), f32),
            pltpu.VMEM((n_sib, chunk, columns), f32),
        ]
        for n in (n_sib, n_leaf, n_sib):
            scratch += [pltpu.SemaphoreType.DMA((n,)), pltpu.SemaphoreType.DMA((n,))]
    vmem = pl.BlockSpec(memory_space=pltpu.VMEM)
    return pl.pallas_call(
        functools.partial(kernel, (n_leaf, n_sib)),
        out_shape=(
            jax.ShapeDtypeStruct((rows, columns), f32),
            jax.ShapeDtypeStruct((rank, columns), f32),
        ),
        in_specs=[pl.BlockSpec(memory_space=pltpu.SMEM)] + [vmem] * 5,
        out_specs=(vmem, vmem),
        scratch_shapes=scratch,
        compiler_params=pltpu.CompilerParams(
            collective_id=0, has_side_effects=True, vmem_limit_bytes=48 * 1024 * 1024
        ),
    )(
        near_index,
        ordering.reshape(leaf_dev, 1, leaf_size),
        sources,
        diagonal_inverse,
        low_rank,
        nearby_blocks,
    )


def solution(mesh):
    placed = (
        P(("leaf", "sib"), None),
        P(("leaf", "sib")),
        P(("leaf", "sib"), None, None),
        P(("leaf", "sib"), None),
        P(("leaf", "sib"), None, None, None),
        P(("leaf", "sib"), None),
    )
    return jax.shard_map(
        on_device,
        mesh=mesh,
        in_specs=placed,
        out_specs=(P(("leaf", "sib"), None), P()),
        check_vma=False,
    )
```

time: 667 us -> 92.3 us (0.14)
  waiting for transfers between devices: 553 us -> 0 us
  Pallas kernels: 0 us -> 84.1 us
  matrix products: 33.6 us -> 0 us
  other arithmetic: 29.7 us -> 0 us
  starting transfers between devices: 18.3 us -> 0 us
  between operations: 14.3 us -> 0.65 us
  local copies, waits for them, and re-layouts: 16.2 us -> 7.22 us
    psum x9 -> x0, waiting for transfers between devices: 550 us -> none  [the longest x4 288 us: totals(): return lax.psum(partner_sum, 'leaf')]
    pallas_call x0 -> x1, Pallas kernels: none -> 84.1 us  [on_device(): pl.pallas_call(functools.partial(kernel, (n_leaf, n_sib)), out_shape=(jax...]
    dot_general x21 -> x0, matrix products: 26.9 us -> none  [the longest x4 8.09 us: on_device(): jnp.einsum('ptog,ptgh->poh', nearby_blocks, piece_list, preferred_element...]
    another operation x5 -> x0, other arithmetic: 22.9 us -> none  [the longest x3 12.4 us: on_device(): jnp.linalg.cholesky(jnp.eye(rank_width, dtype=jnp.float32) + core_sum)]
    ppermute x8 -> x0, starting transfers between devices: 18 us -> none  [the longest x4 12.6 us: with_halo(): before = lax.ppermute(last, axis, up)]
    gather x5 -> x0, local copies, waits for them, and re-layouts: 12 us -> none  [the longest x4 10.3 us: on_device(): piece_list = window[targets]]
  transfers between devices with their start and end apart: 17 -> 0, of which waited for: 12 -> 0; matrix products, arithmetic and copies ran while one was open for 0% -> 0% of each run, Pallas kernels for 0% -> 0%
where the time goes in v1:
time: 92.3 us; the launch traced here: 92 us
  Pallas kernels  84.1 us (91%)
  local copies, waits for them, and re-layouts  7.22 us (8%)
    pallas_call x1, Pallas kernels, on_device(): pl.pallas_call(functools.partial(kernel, (n_leaf, n_sib)), out_shape=(jax...  84.1 us
    unnamed x14, local copies, waits for them, and re-layouts  7.22 us

profile of v1, /device:TPU:0, one launch (start us, length us, event | category | flops | bytes accessed | tf_op | source)
XLA Modules:
  0.0 92.0 jit_solution(13400228227849348241)
XLA Ops:
  0.6 0.0 copy-start
  0.6 1.6 %copy-done = bf16[2,8,256,256]{3,2,1,0:T(8,128)(2,1)S(1)} copy-done((bf16[2,8,256,256]{3,2,1,0:T(8,128)(2,1)S(1)}, bf16[2,8,256,256]{3,2,1,0:T(8,128)(2,1)}, u32[]{:S(2)}) %copy-start) | copy-done | bytes 2097176
  2.2 0.0 copy-start.1
  2.2 1.0 %copy-done.1 = f32[2,256,256]{2,1,0:T(8,128)S(1)} copy-done((f32[2,256,256]{2,1,0:T(8,128)S(1)}, f32[2,256,256]{2,1,0:T(8,128)}, u32[]{:S(2)}) %copy-start.1) | copy-done | bytes 524312
  3.3 0.0 copy-start.2
  3.3 0.9 %copy-done.2 = f32[512,128]{1,0:T(8,128)S(1)} copy-done((f32[512,128]{1,0:T(8,128)S(1)}, f32[512,128]{1,0:T(8,128)}, u32[]{:S(2)}) %copy-start.2) | copy-done | bytes 262168
  4.2 0.0 copy-start.3
  4.2 0.9 %copy-done.3 = f32[512,128]{1,0:T(8,128)S(1)} copy-done((f32[512,128]{1,0:T(8,128)S(1)}, f32[512,128]{1,0:T(8,128)}, u32[]{:S(2)}) %copy-start.3) | copy-done | bytes 262168
  5.2 0.0 copy-start.4
  5.2 0.7 copy-done.4
  5.8 0.0 copy-start.5
  5.9 0.7 copy-done.5
  6.5 84.1 %shard_map.77 = (f32[512,128]{1,0:T(8,128)S(1)}, f32[128,128]{1,0:T(8,128)S(1)}) custom-call(s32[2,8]{1,0:T(2,128)S(1)} %copy-done.5, s32[2,1,256]{2,1,0:T(1,128)S(1)} %bitcast.1, f32[512,128]{1,0:T(8,128)S(1)} %copy-done.2, f32[2,256,256]{2,1,0:T(8,128)S(1)} %copy-done.1, f32[512,128]{1,0:T(8,128)S(1)} %copy-done.3, bf16[2,8,256,256]{3,2,1,0:T(8,128)(2,1)S(1)} %copy-done), custom_call_target="tpu_custom_call" | custom-call | tf_op jit(solution)/shard_map/pallas_call | solution.py:320
  90.6 0.7 copy.10
  91.4 0.6 copy.11
Async XLA Ops:
  0.6 1.6 %copy-start = (bf16[2,8,256,256]{3,2,1,0:T(8,128)(2,1)S(1)}, bf16[2,8,256,256]{3,2,1,0:T(8,128)(2,1)}, u32[]{:S(2)}) copy-start(bf16[2,8,256,256]{3,2,1,0:T(8,128)(2,1)} %nearby.1) | copy-start | bytes 6291460
  2.2 1.0 %copy-start.1 = (f32[2,256,256]{2,1,0:T(8,128)S(1)}, f32[2,256,256]{2,1,0:T(8,128)}, u32[]{:S(2)}) copy-start(f32[2,256,256]{2,1,0:T(8,128)} %diag.1) | copy-start | bytes 1572868
  3.3 0.9 %copy-start.2 = (f32[512,128]{1,0:T(8,128)S(1)}, f32[512,128]{1,0:T(8,128)}, u32[]{:S(2)}) copy-start(f32[512,128]{1,0:T(8,128)} %src.1) | copy-start | bytes 786436
  4.2 0.9 %copy-start.3 = (f32[512,128]{1,0:T(8,128)S(1)}, f32[512,128]{1,0:T(8,128)}, u32[]{:S(2)}) copy-start(f32[512,128]{1,0:T(8,128)} %low.1) | copy-start | bytes 786436
  5.2 0.7 copy-start.4
  5.8 0.7 copy-start.5

commit v2 on v1

v2 whole, which is shorter than its diff:
```python
import functools

import jax
import jax.numpy as jnp
from jax import lax
from jax.experimental import pallas as pl
from jax.experimental.pallas import tpu as pltpu
from jax.sharding import PartitionSpec as P

ITERS = 4
MESH = pl.DeviceIdType.MESH
HIGH = lax.Precision.HIGHEST
COUNTS = (2, 2, 2) + (1,) * ITERS
PIVOTS = 8
LEVELS = 5


def mm(a, b):
    return jnp.dot(a, b, precision=HIGH, preferred_element_type=jnp.float32)


def mm_t(a, b):
    return lax.dot_general(
        a, b, (((0,), (0,)), ((), ())), precision=HIGH, preferred_element_type=jnp.float32
    )


def split(x):
    high = x.astype(jnp.bfloat16)
    return high, (x - high.astype(jnp.float32)).astype(jnp.bfloat16)


def guess(core, right):
    size = core.shape[0]
    eye = lax.broadcasted_iota(jnp.int32, (size, size), 0) == lax.broadcasted_iota(
        jnp.int32, (size, size), 1
    )
    bound = jnp.max(jnp.sum(jnp.abs(core), axis=1, keepdims=True), axis=0, keepdims=True)
    scale = 2.0 / (1.0 + bound)
    rest = jnp.where(eye, 1.0, 0.0) - core * scale
    value = right * scale
    for level in range(LEVELS):
        value += jnp.dot(rest, value, preferred_element_type=jnp.float32)
        if level + 1 < LEVELS:
            rest = jnp.dot(rest, rest, preferred_element_type=jnp.float32)
    return value


def eliminate(work, offsets):
    size = work.shape[0]
    lane = lax.broadcasted_iota(jnp.int32, (PIVOTS, size), 1)
    sub = lax.broadcasted_iota(jnp.int32, (PIVOTS, size), 0)
    wide = lax.broadcasted_iota(jnp.int32, (size, size), 1)
    for off in offsets:
        panel = work[off : off + PIVOTS, :]
        left = jnp.where(lane < off, -panel, panel)
        for j in range(PIVOTS):
            c = off + j
            inv = 1.0 / panel[j : j + 1, c : c + 1]
            row = jnp.where(lane == c, inv, panel[j : j + 1, :] * inv)
            rest = jnp.where(lane == c, 0.0, panel) - panel[:, c : c + 1] * row
            panel = jnp.where(sub == j, row, rest)
        inside = (wide >= off) & (wide < off + PIVOTS)
        work[...] = jnp.where(inside, 0.0, work[...]) - mm_t(left, panel)
        work[off : off + PIVOTS, :] = panel


def parted(n, sizes, last):
    n_leaf, n_sib = sizes
    return not last and (n // n_sib) % n_leaf == 0


class Sum:
    def __init__(self, me, sizes, refs):
        self.leaf, self.sib = me
        self.n_leaf, self.n_sib = sizes
        self.src, self.r1, self.t2, self.r2, self.r3, *self.sems = refs
        self.chunk = self.r1.shape[1]
        self.parts, self.piece = self.r3.shape[1:3]
        self.open, self.now = [], []
        self.steps = [self.scatter_sib]
        if self.parts > 1:
            self.steps += [self.scatter_leaf, self.gather_leaf, self.gather_sib]
        else:
            self.steps += [self.exchange_leaf, self.gather_sib]

    def step(self):
        if self.steps:
            work, self.steps = self.steps[0], self.steps[1:]
            work()

    def arrived(self):
        for c in self.now:
            c.wait_recv()
        self.now = []

    def copy(self, src, dst, phase, o, target):
        send, recv = self.sems[2 * phase], self.sems[2 * phase + 1]
        c = pltpu.make_async_remote_copy(
            src_ref=src, dst_ref=dst, send_sem=send.at[o], recv_sem=recv.at[o],
            device_id=target, device_id_type=MESH,
        )
        c.start()
        self.open.append(c)
        self.now.append(c)

    def sibs(self):
        for o in range(1, self.n_sib):
            to = lax.rem(self.sib + o, self.n_sib)
            yield o, to, (self.leaf, to)

    def leaves(self):
        for o in range(1, self.n_leaf):
            to = lax.rem(self.leaf + o, self.n_leaf)
            yield o, to, (to, self.sib)

    def scatter_sib(self):
        for o, to, place in self.sibs():
            rows = pl.ds(pl.multiple_of(to * self.chunk, 8), self.chunk)
            self.copy(self.src.at[rows], self.r1.at[o], 0, o, place)

    def own(self):
        rows = pl.ds(pl.multiple_of(self.sib * self.chunk, 8), self.chunk)
        total = self.src[rows, :]
        self.arrived()
        for o in range(1, self.n_sib):
            total += self.r1[o]
        return total

    def exchange_leaf(self):
        self.r2[self.leaf] = self.own()
        mine = self.r2.at[self.leaf]
        for o, to, place in self.leaves():
            self.copy(mine, mine, 1, o, place)

    def scatter_leaf(self):
        total = self.own()
        for o in range(self.n_leaf):
            self.t2[o] = total[o * self.piece : (o + 1) * self.piece]
        for o, to, place in self.leaves():
            self.copy(self.t2.at[to], self.r2.at[o], 1, o, place)

    def gather_leaf(self):
        self.arrived()
        total = self.t2[self.leaf]
        for o in range(1, self.n_leaf):
            total += self.r2[o]
        self.r3[self.sib, self.leaf] = total
        mine = self.r3.at[self.sib, self.leaf]
        for o, to, place in self.leaves():
            self.copy(mine, mine, 2, o, place)

    def gather_sib(self):
        self.arrived()
        if self.parts == 1:
            total = self.r2[0]
            for o in range(1, self.n_leaf):
                total += self.r2[o]
            self.r3[self.sib, 0] = total
        mine = self.r3.at[self.sib]
        for o, to, place in self.sibs():
            self.copy(mine, mine, 3, o, place)

    def result(self):
        while self.steps:
            self.step()
        self.arrived()
        return jnp.concatenate(
            [self.r3[s, l] for s in range(self.n_sib) for l in range(self.parts)], axis=0
        )


def kernel(
    sizes, near_in, order_in, src_in, diag_in, low_in, nearby_in, sol, coef, *scratch
):
    n_leaf, n_sib = sizes
    leaf, sib = lax.axis_index("leaf"), lax.axis_index("sib")
    pos = leaf * n_sib + sib
    last = n_leaf * n_sib - 1
    (near, order, src, diag, low, nearby), in_sem, scratch = scratch[:6], scratch[6], scratch[7:]
    loads = [
        pltpu.make_async_copy(a, b, in_sem.at[i])
        for i, (a, b) in enumerate(
            ((low_in, low), (diag_in, diag), (order_in, order), (src_in, src),
             (near_in, near), (nearby_in, nearby))
        )
    ]
    for c in loads:
        c.start()
    leaf_dev, leaf_size = diag.shape[0], diag.shape[1]
    rank = low.shape[1]
    columns = src.shape[1]
    blocks = [slice(i * leaf_size, (i + 1) * leaf_size) for i in range(leaf_dev)]
    windows, scratch = scratch[: 2 * ITERS], scratch[2 * ITERS :]
    h_send, h_recv, lifted, lifted_t, powers, x_first, work, d_high, d_low = scratch[:9]
    scratch = scratch[9:]
    sums = [Sum((leaf, sib), sizes, scratch[13 * i : 13 * i + 13]) for i in range(len(COUNTS))]
    moment_sums, image_sums = sums[1:3], sums[3:]

    def place(p):
        return (p // n_sib, lax.rem(p, n_sib))

    right, left = place(jnp.minimum(pos + 1, last)), place(jnp.maximum(pos - 1, 0))
    has_right, has_left = pos < last, pos > 0

    barrier = pltpu.get_barrier_semaphore()
    for o in range(1, n_sib):
        pl.semaphore_signal(
            barrier, inc=1, device_id=(leaf, lax.rem(sib + o, n_sib)), device_id_type=MESH
        )
    for o in range(1, n_leaf):
        pl.semaphore_signal(
            barrier, inc=1, device_id=(lax.rem(leaf + o, n_leaf), sib), device_id_type=MESH
        )

    @pl.when(has_right)
    def _():
        pl.semaphore_signal(barrier, inc=1, device_id=right, device_id_type=MESH)

    @pl.when(has_left)
    def _():
        pl.semaphore_signal(barrier, inc=1, device_id=left, device_id_type=MESH)

    def halo(k):
        own = windows[k].at[leaf_dev : 2 * leaf_dev]
        up = pltpu.make_async_remote_copy(
            src_ref=own, dst_ref=windows[k].at[0:leaf_dev],
            send_sem=h_send.at[k, 0], recv_sem=h_recv.at[k, 0],
            device_id=right, device_id_type=MESH,
        )
        down = pltpu.make_async_remote_copy(
            src_ref=own, dst_ref=windows[k].at[2 * leaf_dev : 3 * leaf_dev],
            send_sem=h_send.at[k, 1], recv_sem=h_recv.at[k, 1],
            device_id=left, device_id_type=MESH,
        )
        return up, down

    def send_halo(k, values):
        for i in range(leaf_dev):
            windows[k][leaf_dev + i] = values[i].astype(jnp.bfloat16)
        up, down = halo(k)
        pl.when(has_right)(lambda: up.start())
        pl.when(has_left)(lambda: down.start())

    def wait_halo(k):
        up, down = halo(k)
        pl.when(has_left)(lambda: up.wait_recv())
        pl.when(has_right)(lambda: down.wait_recv())

    def near_apply(k):
        out = []
        for i in range(leaf_dev):
            total = None
            for m in range(near.shape[1]):
                t = jnp.clip(near[i, m] - (pos - 1) * leaf_dev, 0, 3 * leaf_dev - 1)
                part = jnp.dot(nearby[i, m], windows[k][t], preferred_element_type=jnp.float32)
                total = part if total is None else total + part
            out.append(total)
        return out

    def project(values):
        return sum(mm(lifted_t[:, blocks[i]], values[i]) for i in range(leaf_dev))

    def inverse_times(i, v):
        high, rest = split(v)
        wide = jnp.dot(
            d_high[i], jnp.concatenate([high, rest], axis=1), preferred_element_type=jnp.float32
        )
        small = jnp.dot(d_low[i], high, preferred_element_type=jnp.float32)
        return wide[:, : v.shape[1]] + (wide[:, v.shape[1] :] + small)

    core = jnp.zeros((rank, rank), jnp.float32)
    first = jnp.zeros((rank, columns), jnp.float32)
    row_ids = lax.broadcasted_iota(jnp.int32, (leaf_size, leaf_size), 0)
    loads[0].wait()
    loads[1].wait()
    for i, rows in enumerate(blocks):
        d_high[i], d_low[i] = split(diag[i])
        block = low[rows, :]
        up = mm(diag[i], block)
        lifted[rows, :] = up
        up_t = up.T
        lifted_t[:, rows] = up_t
        core += mm(up_t, block)
    loads[2].wait()
    loads[3].wait()
    scaled = []
    for i, rows in enumerate(blocks):
        local = order[i] - (pos * leaf_dev + i) * leaf_size
        pick = (row_ids == local).astype(jnp.float32).T.astype(jnp.bfloat16)
        value = src[rows, :]
        high = value.astype(jnp.bfloat16)
        value = value - high.astype(jnp.float32)
        parts = jnp.concatenate([high, *split(value)], axis=1)
        parts = jnp.dot(pick, parts, preferred_element_type=jnp.float32)
        ordered = parts[:, :columns] + (
            parts[:, columns : 2 * columns] + parts[:, 2 * columns :]
        )
        scaled.append(inverse_times(i, ordered))
        first += mm(lifted_t[:, rows], ordered)
    sums[0].src[0:rank, :] = core
    sums[0].src[rank:, :] = first

    sides = 1 - pos // last + (pos + last - 1) // last
    pl.semaphore_wait(barrier, n_sib + n_leaf - 2 + sides)

    sums[0].step()
    send_halo(0, [lifted[rows, :] for rows in blocks])
    loads[4].wait()
    loads[5].wait()

    def power(j):
        wait_halo(j)
        image = near_apply(j)
        value = [-inverse_times(i, image[i]) for i in range(leaf_dev)]
        if j + 1 < ITERS:
            send_halo(j + 1, value)
        for i, rows in enumerate(blocks):
            powers[j, rows, :] = value[i]
        part = j % 2
        moment_sums[j // 2].src[part * rank : (part + 1) * rank, :] = project(image)
        if part:
            moment_sums[j // 2].step()

    sums[0].step()
    sums[0].step()
    power(0)
    both = sums[0].result()
    eye = lax.broadcasted_iota(jnp.int32, (rank, rank), 0) == lax.broadcasted_iota(
        jnp.int32, (rank, rank), 1
    )
    core = both[:rank] + jnp.where(eye, 1.0, 0.0)
    first = both[rank:]
    base = ITERS
    start = guess(core, first)
    now = []
    for i, rows in enumerate(blocks):
        value = scaled[i] - mm(lifted[rows, :], start)
        x_first[rows, :] = value
        now.append(value)
    send_halo(base, now)
    work[...] = core
    steps = list(range(0, rank, PIVOTS))
    share = len(steps) // ITERS

    power(1)
    eliminate(work, steps[:share])
    for k in range(ITERS):
        wait_halo(base + k)
        image = near_apply(base + k)
        now = [x_first[rows, :] - inverse_times(i, image[i]) for i, rows in enumerate(blocks)]
        if k + 1 < ITERS:
            send_halo(base + k + 1, now)
        image_sums[k].src[...] = project(image)
        image_sums[k].step()
        moment_sums[0].step()
        for j in range(k):
            image_sums[j].step()
        if k >= 2:
            moment_sums[1].step()
        if k + 2 < ITERS:
            power(k + 2)
        if k + 1 < ITERS:
            end = (k + 2) * share if k + 2 < ITERS else len(steps)
            eliminate(work, steps[(k + 1) * share : end])

    inverse = work[...]
    deltas = [mm(inverse, first) - start]
    moments = moment_sums[0].result()
    moment = [moments[:rank], moments[rank:]]

    def known(k):
        return sum(mm(moment[j], deltas[k - 1 - j]) for j in range(k))

    def solve(k):
        deltas.append(deltas[0] + mm(inverse, known(k) - image_sums[k - 1].result()))

    solve(1)
    image_sums[-1].step()
    for s in (moment_sums[1], *image_sums[1:-1]):
        s.step()
    solve(2)
    image_sums[-1].step()
    moments = moment_sums[1].result()
    moment += [moments[:rank], moments[rank:]]
    solve(3)

    def correct(i, j):
        basis = lifted[blocks[i], :] if j == 0 else powers[j - 1, blocks[i], :]
        return mm(basis, deltas[ITERS - j])

    now = [now[i] - sum(correct(i, j) for j in range(1, ITERS + 1)) for i in range(leaf_dev)]
    solve(4)
    for i, rows in enumerate(blocks):
        sol[rows, :] = now[i] - correct(i, 0)
    coef[...] = start + deltas[ITERS]

    for s in sums:
        for c in s.open:
            c.wait_send()
    for k in range(2 * ITERS):
        up, down = halo(k)
        pl.when(has_right)(lambda up=up: up.wait_send())
        pl.when(has_left)(lambda down=down: down.wait_send())


def on_device(sources, ordering, diagonal_inverse, low_rank, nearby_blocks, near_index):
    n_leaf, n_sib = lax.axis_size("leaf"), lax.axis_size("sib")
    leaf_dev, leaf_size = diagonal_inverse.shape[:2]
    rows, columns = sources.shape
    rank = low_rank.shape[1]
    f32 = jnp.float32
    operands = (
        near_index,
        ordering.reshape(leaf_dev, 1, leaf_size),
        sources,
        diagonal_inverse,
        low_rank,
        nearby_blocks,
    )
    scratch = [pltpu.SMEM(near_index.shape, near_index.dtype)]
    scratch += [pltpu.VMEM(x.shape, x.dtype) for x in operands[1:]]
    scratch += [pltpu.SemaphoreType.DMA((len(operands),))]
    scratch += [
        pltpu.VMEM((3 * leaf_dev, leaf_size, columns), jnp.bfloat16) for _ in range(2 * ITERS)
    ]
    scratch += [
        pltpu.SemaphoreType.DMA((2 * ITERS, 2)),
        pltpu.SemaphoreType.DMA((2 * ITERS, 2)),
        pltpu.VMEM((rows, rank), f32),
        pltpu.VMEM((rank, rows), f32),
        pltpu.VMEM((ITERS, rows, rank), f32),
        pltpu.VMEM((rows, columns), f32),
        pltpu.VMEM((rank, rank), f32),
        pltpu.VMEM(diagonal_inverse.shape, jnp.bfloat16),
        pltpu.VMEM(diagonal_inverse.shape, jnp.bfloat16),
    ]
    for n, count in enumerate(COUNTS):
        total = count * rank
        chunk = total // n_sib
        cut = parted(total, (n_leaf, n_sib), n + 1 == len(COUNTS))
        parts = n_leaf if cut else 1
        piece = chunk // parts
        scratch += [
            pltpu.VMEM((total, columns), f32),
            pltpu.VMEM((n_sib, chunk, columns), f32),
            pltpu.VMEM((parts, piece, columns), f32),
            pltpu.VMEM((n_leaf, piece, columns), f32),
            pltpu.VMEM((n_sib, parts, piece, columns), f32),
        ]
        for n in (n_sib, n_leaf, n_leaf, n_sib):
            scratch += [pltpu.SemaphoreType.DMA((n,)), pltpu.SemaphoreType.DMA((n,))]
    vmem = pl.BlockSpec(memory_space=pltpu.VMEM)
    return pl.pallas_call(
        functools.partial(kernel, (n_leaf, n_sib)),
        out_shape=(
            jax.ShapeDtypeStruct((rows, columns), f32),
            jax.ShapeDtypeStruct((rank, columns), f32),
        ),
        in_specs=[pl.BlockSpec(memory_space=pl.ANY)] * len(operands),
        out_specs=(vmem, vmem),
        scratch_shapes=scratch,
        compiler_params=pltpu.CompilerParams(
            collective_id=0, has_side_effects=True, vmem_limit_bytes=62 * 1024 * 1024
        ),
    )(*operands)


def solution(mesh):
    placed = (
        P(("leaf", "sib"), None),
        P(("leaf", "sib")),
        P(("leaf", "sib"), None, None),
        P(("leaf", "sib"), None),
        P(("leaf", "sib"), None, None, None),
        P(("leaf", "sib"), None),
    )
    return jax.shard_map(
        on_device,
        mesh=mesh,
        in_specs=placed,
        out_specs=(P(("leaf", "sib"), None), P()),
        check_vma=False,
    )
```

time: 92.3 us -> 76.4 us (0.83)
  Pallas kernels: 84.1 us -> 72.4 us
  local copies, waits for them, and re-layouts: 7.22 us -> 3.14 us
    pallas_call x1, Pallas kernels: 84.1 us -> 72.4 us  [on_device(): pl.pallas_call(functools.partial(kernel, (n_leaf, n_sib)), out_shape=(jax...]
    unnamed x14 -> x2, local copies, waits for them, and re-layouts: 7.22 us -> 3.14 us
where the time goes in v2:
time: 76.4 us; the launch traced here: 76.2 us
  Pallas kernels  72.4 us (95%)
  local copies, waits for them, and re-layouts  3.14 us (4%)
    pallas_call x1, Pallas kernels, on_device(): pl.pallas_call(functools.partial(kernel, (n_leaf, n_sib)), out_shape=(jax...  72.4 us
    unnamed x2, local copies, waits for them, and re-layouts  3.14 us

profile of v2, /device:TPU:0, one launch (start us, length us, event | category | flops | bytes accessed | tf_op | source)
XLA Modules:
  0.0 76.2 jit_solution(8407971312234706576)
XLA Ops:
  0.6 72.4 %shard_map.77 = (f32[512,128]{1,0:T(8,128)}, f32[128,128]{1,0:T(8,128)}) custom-call(s32[2,8]{1,0:T(2,128)} %near_in.1, s32[2,1,256]{2,1,0:T(1,128)} %bitcast.1, f32[512,128]{1,0:T(8,128)} %src_in.1, f32[2,256,256]{2,1,0:T(8,128)} %diag_in.1, f32[512,128]{1,0:T(8,128)} %low_in.1, bf16[2,8,256,256]{3,2,1,0:T(8,128)(2,1)} %nearby_in.1), custom_call_target="tpu_custom_call" | custom-call | tf_op jit(solution)/shard_map/pallas_call | solution.py:454
  73.0 1.7 %copy.10 = f32[512,128]{1,0:T(8,128)} copy(f32[512,128]{1,0:T(8,128)} %get-tuple-element.4) | data formatting | bytes 524288
  74.7 1.5 %copy.11 = f32[128,128]{1,0:T(8,128)} copy(f32[128,128]{1,0:T(8,128)} %get-tuple-element.5) | data formatting | bytes 131072

commit v3 on v2

--- a/solution.py
+++ b/solution.py
@@ -11,7 +11,7 @@
 MESH = pl.DeviceIdType.MESH
 HIGH = lax.Precision.HIGHEST
 COUNTS = (2, 2, 2) + (1,) * ITERS
-PIVOTS = 8
+PIVOTS = 16
 LEVELS = 5
 
 
@@ -46,6 +46,11 @@
     return value
 
 
+def split3(x):
+    high = x.astype(jnp.bfloat16)
+    return (high, *split(x - high.astype(jnp.float32)))
+
+
 def eliminate(work, offsets):
     size = work.shape[0]
     lane = lax.broadcasted_iota(jnp.int32, (PIVOTS, size), 1)
@@ -54,14 +59,27 @@
     for off in offsets:
         panel = work[off : off + PIVOTS, :]
         left = jnp.where(lane < off, -panel, panel)
+        cols = [
+            jnp.broadcast_to(panel[:, off + j : off + j + 1], panel.shape) for j in range(PIVOTS)
+        ]
+        inside = (lane >= off) & (lane < off + PIVOTS)
+        panel = jnp.where(inside, jnp.where(lane == off + sub, 1.0, 0.0), panel)
         for j in range(PIVOTS):
-            c = off + j
-            inv = 1.0 / panel[j : j + 1, c : c + 1]
-            row = jnp.where(lane == c, inv, panel[j : j + 1, :] * inv)
-            rest = jnp.where(lane == c, 0.0, panel) - panel[:, c : c + 1] * row
-            panel = jnp.where(sub == j, row, rest)
+            inv = 1.0 / cols[j][j : j + 1, :]
+            row = panel[j : j + 1, :] * inv
+            panel = jnp.where(sub == j, row, panel - cols[j] * row)
+            for m in range(j + 1, PIVOTS):
+                row = cols[m][j : j + 1, :] * inv
+                cols[m] = jnp.where(sub == j, row, cols[m] - cols[j] * row)
+        h, m, l = split3(left.T)
+        rh, rm, rl = split3(panel)
+        update = jnp.dot(
+            jnp.concatenate([h, h, m, h, l, m], axis=1),
+            jnp.concatenate([rh, rm, rh, rl, rh, rm], axis=0),
+            preferred_element_type=jnp.float32,
+        )
         inside = (wide >= off) & (wide < off + PIVOTS)
-        work[...] = jnp.where(inside, 0.0, work[...]) - mm_t(left, panel)
+        work[...] = jnp.where(inside, 0.0, work[...]) - update
         work[off : off + PIVOTS, :] = panel
 
 
@@ -221,42 +239,44 @@
     def _():
         pl.semaphore_signal(barrier, inc=1, device_id=left, device_id_type=MESH)
 
-    def halo(k):
-        own = windows[k].at[leaf_dev : 2 * leaf_dev]
+    def halo(k, i):
+        own = windows[k].at[leaf_dev + i]
         up = pltpu.make_async_remote_copy(
-            src_ref=own, dst_ref=windows[k].at[0:leaf_dev],
-            send_sem=h_send.at[k, 0], recv_sem=h_recv.at[k, 0],
+            src_ref=own, dst_ref=windows[k].at[i],
+            send_sem=h_send.at[k, 0, i], recv_sem=h_recv.at[k, 0, i],
             device_id=right, device_id_type=MESH,
         )
         down = pltpu.make_async_remote_copy(
-            src_ref=own, dst_ref=windows[k].at[2 * leaf_dev : 3 * leaf_dev],
-            send_sem=h_send.at[k, 1], recv_sem=h_recv.at[k, 1],
+            src_ref=own, dst_ref=windows[k].at[2 * leaf_dev + i],
+            send_sem=h_send.at[k, 1, i], recv_sem=h_recv.at[k, 1, i],
             device_id=left, device_id_type=MESH,
         )
         return up, down
 
-    def send_halo(k, values):
-        for i in range(leaf_dev):
-            windows[k][leaf_dev + i] = values[i].astype(jnp.bfloat16)
-        up, down = halo(k)
+    def send_block(k, i, value):
+        windows[k][leaf_dev + i] = value.astype(jnp.bfloat16)
+        up, down = halo(k, i)
         pl.when(has_right)(lambda: up.start())
         pl.when(has_left)(lambda: down.start())
 
     def wait_halo(k):
-        up, down = halo(k)
-        pl.when(has_left)(lambda: up.wait_recv())
-        pl.when(has_right)(lambda: down.wait_recv())
-
-    def near_apply(k):
-        out = []
-        for i in range(leaf_dev):
-            total = None
-            for m in range(near.shape[1]):
-                t = jnp.clip(near[i, m] - (pos - 1) * leaf_dev, 0, 3 * leaf_dev - 1)
-                part = jnp.dot(nearby[i, m], windows[k][t], preferred_element_type=jnp.float32)
-                total = part if total is None else total + part
-            out.append(total)
-        return out
+        @pl.when(has_left)
+        def _():
+            for i in range(leaf_dev):
+                halo(k, i)[0].wait_recv()
+
+        @pl.when(has_right)
+        def _():
+            for i in range(leaf_dev):
+                halo(k, i)[1].wait_recv()
+
+    def near_apply(k, i):
+        total = None
+        for m in range(near.shape[1]):
+            t = jnp.clip(near[i, m] - (pos - 1) * leaf_dev, 0, 3 * leaf_dev - 1)
+            part = jnp.dot(nearby[i, m], windows[k][t], preferred_element_type=jnp.float32)
+            total = part if total is None else total + part
+        return total
 
     def project(values):
         return sum(mm(lifted_t[:, blocks[i]], values[i]) for i in range(leaf_dev))
@@ -282,6 +302,10 @@
         up_t = up.T
         lifted_t[:, rows] = up_t
         core += mm(up_t, block)
+    sides = 1 - pos // last + (pos + last - 1) // last
+    pl.semaphore_wait(barrier, n_sib + n_leaf - 2 + sides)
+    for i, rows in enumerate(blocks):
+        send_block(0, i, lifted[rows, :])
     loads[2].wait()
     loads[3].wait()
     scaled = []
@@ -301,22 +325,19 @@
     sums[0].src[0:rank, :] = core
     sums[0].src[rank:, :] = first
 
-    sides = 1 - pos // last + (pos + last - 1) // last
-    pl.semaphore_wait(barrier, n_sib + n_leaf - 2 + sides)
-
     sums[0].step()
-    send_halo(0, [lifted[rows, :] for rows in blocks])
     loads[4].wait()
     loads[5].wait()
 
     def power(j):
         wait_halo(j)
-        image = near_apply(j)
-        value = [-inverse_times(i, image[i]) for i in range(leaf_dev)]
-        if j + 1 < ITERS:
-            send_halo(j + 1, value)
+        image = []
         for i, rows in enumerate(blocks):
-            powers[j, rows, :] = value[i]
+            image.append(near_apply(j, i))
+            value = -inverse_times(i, image[i])
+            powers[j, rows, :] = value
+            if j + 1 < ITERS:
+                send_block(j + 1, i, value)
         part = j % 2
         moment_sums[j // 2].src[part * rank : (part + 1) * rank, :] = project(image)
         if part:
@@ -336,9 +357,9 @@
     now = []
     for i, rows in enumerate(blocks):
         value = scaled[i] - mm(lifted[rows, :], start)
+        send_block(base, i, value)
         x_first[rows, :] = value
         now.append(value)
-    send_halo(base, now)
     work[...] = core
     steps = list(range(0, rank, PIVOTS))
     share = len(steps) // ITERS
@@ -347,10 +368,12 @@
     eliminate(work, steps[:share])
     for k in range(ITERS):
         wait_halo(base + k)
-        image = near_apply(base + k)
-        now = [x_first[rows, :] - inverse_times(i, image[i]) for i, rows in enumerate(blocks)]
-        if k + 1 < ITERS:
-            send_halo(base + k + 1, now)
+        image, now = [], []
+        for i, rows in enumerate(blocks):
+            image.append(near_apply(base + k, i))
+            now.append(x_first[rows, :] - inverse_times(i, image[i]))
+            if k + 1 < ITERS:
+                send_block(base + k + 1, i, now[i])
         image_sums[k].src[...] = project(image)
         image_sums[k].step()
         moment_sums[0].step()
@@ -385,23 +408,27 @@
     moment += [moments[:rank], moments[rank:]]
     solve(3)
 
-    def correct(i, j):
-        basis = lifted[blocks[i], :] if j == 0 else powers[j - 1, blocks[i], :]
-        return mm(basis, deltas[ITERS - j])
-
-    now = [now[i] - sum(correct(i, j) for j in range(1, ITERS + 1)) for i in range(leaf_dev)]
-    solve(4)
+    part = deltas[0] + mm(inverse, known(ITERS))
+    deltas.append(part)
     for i, rows in enumerate(blocks):
-        sol[rows, :] = now[i] - correct(i, 0)
-    coef[...] = start + deltas[ITERS]
+        value = now[i] - mm(lifted[rows, :], part)
+        for j in range(1, ITERS + 1):
+            value -= mm(powers[j - 1, rows, :], deltas[ITERS - j])
+        sol[rows, :] = value
+        lifted[rows, :] = mm(lifted[rows, :], inverse)
+    final = image_sums[-1].result()
+    for rows in blocks:
+        sol[rows, :] += mm(lifted[rows, :], final)
+    coef[...] = start + part - mm(inverse, final)
 
     for s in sums:
         for c in s.open:
             c.wait_send()
     for k in range(2 * ITERS):
-        up, down = halo(k)
-        pl.when(has_right)(lambda up=up: up.wait_send())
-        pl.when(has_left)(lambda down=down: down.wait_send())
+        for i in range(leaf_dev):
+            up, down = halo(k, i)
+            pl.when(has_right)(lambda up=up: up.wait_send())
+            pl.when(has_left)(lambda down=down: down.wait_send())
 
 
 def on_device(sources, ordering, diagonal_inverse, low_rank, nearby_blocks, near_index):
@@ -425,8 +452,8 @@
         pltpu.VMEM((3 * leaf_dev, leaf_size, columns), jnp.bfloat16) for _ in range(2 * ITERS)
     ]
     scratch += [
-        pltpu.SemaphoreType.DMA((2 * ITERS, 2)),
-        pltpu.SemaphoreType.DMA((2 * ITERS, 2)),
+        pltpu.SemaphoreType.DMA((2 * ITERS, 2, leaf_dev)),
+        pltpu.SemaphoreType.DMA((2 * ITERS, 2, leaf_dev)),
         pltpu.VMEM((rows, rank), f32),
         pltpu.VMEM((rank, rows), f32),
         pltpu.VMEM((ITERS, rows, rank), f32),

time: 76.4 us -> 75.2 us (0.984)
  Pallas kernels: 72.4 us -> 71.2 us
    pallas_call x1, Pallas kernels: 72.4 us -> 71.2 us  [on_device(): pl.pallas_call(functools.partial(kernel, (n_leaf, n_sib)), out_shape=(jax...]
where the time goes in v3:
time: 75.2 us; the launch traced here: 75 us
  Pallas kernels  71.2 us (95%)
  local copies, waits for them, and re-layouts  3.14 us (4%)
    pallas_call x1, Pallas kernels, on_device(): pl.pallas_call(functools.partial(kernel, (n_leaf, n_sib)), out_shape=(jax...  71.2 us
    unnamed x2, local copies, waits for them, and re-layouts  3.14 us

profile of v3, /device:TPU:0, one launch (start us, length us, event | category | flops | bytes accessed | tf_op | source)
XLA Modules:
  0.0 75.0 jit_solution(6977134917607233513)
XLA Ops:
  0.6 71.2 %shard_map.77 = (f32[512,128]{1,0:T(8,128)}, f32[128,128]{1,0:T(8,128)}) custom-call(s32[2,8]{1,0:T(2,128)} %near_in.1, s32[2,1,256]{2,1,0:T(1,128)} %bitcast.1, f32[512,128]{1,0:T(8,128)} %src_in.1, f32[2,256,256]{2,1,0:T(8,128)} %diag_in.1, f32[512,128]{1,0:T(8,128)} %low_in.1, bf16[2,8,256,256]{3,2,1,0:T(8,128)(2,1)} %nearby_in.1), custom_call_target="tpu_custom_call" | custom-call | tf_op jit(solution)/shard_map/pallas_call | solution.py:481
  71.8 1.7 %copy.10 = f32[512,128]{1,0:T(8,128)} copy(f32[512,128]{1,0:T(8,128)} %get-tuple-element.4) | data formatting | bytes 524288
  73.5 1.5 %copy.11 = f32[128,128]{1,0:T(8,128)} copy(f32[128,128]{1,0:T(8,128)} %get-tuple-element.5) | data formatting | bytes 131072

commit v4 on v3

--- a/solution.py
+++ b/solution.py
@@ -10,7 +10,7 @@
 ITERS = 4
 MESH = pl.DeviceIdType.MESH
 HIGH = lax.Precision.HIGHEST
-COUNTS = (2, 2, 2) + (1,) * ITERS
+COUNTS = (2, ITERS, 2, 2)
 PIVOTS = 16
 LEVELS = 5
 
@@ -83,19 +83,19 @@
         work[off : off + PIVOTS, :] = panel
 
 
-def parted(n, sizes, last):
+def parted(n, sizes):
     n_leaf, n_sib = sizes
-    return not last and (n // n_sib) % n_leaf == 0
+    return (n // n_sib) % n_leaf == 0
 
 
 class Sum:
     def __init__(self, me, sizes, refs):
         self.leaf, self.sib = me
         self.n_leaf, self.n_sib = sizes
-        self.src, self.r1, self.t2, self.r2, self.r3, *self.sems = refs
+        self.src, self.r1, self.t2, self.r2, self.r3, self.send, self.recv = refs
         self.chunk = self.r1.shape[1]
         self.parts, self.piece = self.r3.shape[1:3]
-        self.open, self.now = [], []
+        self.open, self.now = [], None
         self.steps = [self.scatter_sib]
         if self.parts > 1:
             self.steps += [self.scatter_leaf, self.gather_leaf, self.gather_sib]
@@ -108,19 +108,23 @@
             work()
 
     def arrived(self):
-        for c in self.now:
-            c.wait_recv()
-        self.now = []
-
-    def copy(self, src, dst, phase, o, target):
-        send, recv = self.sems[2 * phase], self.sems[2 * phase + 1]
-        c = pltpu.make_async_remote_copy(
-            src_ref=src, dst_ref=dst, send_sem=send.at[o], recv_sem=recv.at[o],
+        phase, bulk = self.now
+        pltpu.make_async_copy(bulk, bulk, self.recv.at[phase]).wait()
+
+    def sent(self):
+        for phase, bulk in self.open:
+            pltpu.make_async_copy(bulk, bulk, self.send.at[phase]).wait()
+        self.open = []
+
+    def bulk(self, phase, ref):
+        self.now = (phase, ref)
+        self.open.append(self.now)
+
+    def copy(self, src, dst, phase, target):
+        pltpu.make_async_remote_copy(
+            src_ref=src, dst_ref=dst, send_sem=self.send.at[phase], recv_sem=self.recv.at[phase],
             device_id=target, device_id_type=MESH,
-        )
-        c.start()
-        self.open.append(c)
-        self.now.append(c)
+        ).start()
 
     def sibs(self):
         for o in range(1, self.n_sib):
@@ -135,7 +139,8 @@
     def scatter_sib(self):
         for o, to, place in self.sibs():
             rows = pl.ds(pl.multiple_of(to * self.chunk, 8), self.chunk)
-            self.copy(self.src.at[rows], self.r1.at[o], 0, o, place)
+            self.copy(self.src.at[rows], self.r1.at[o], 0, place)
+        self.bulk(0, self.r1.at[1:])
 
     def own(self):
         rows = pl.ds(pl.multiple_of(self.sib * self.chunk, 8), self.chunk)
@@ -149,14 +154,16 @@
         self.r2[self.leaf] = self.own()
         mine = self.r2.at[self.leaf]
         for o, to, place in self.leaves():
-            self.copy(mine, mine, 1, o, place)
+            self.copy(mine, mine, 1, place)
+        self.bulk(1, self.r2.at[1:])
 
     def scatter_leaf(self):
         total = self.own()
         for o in range(self.n_leaf):
             self.t2[o] = total[o * self.piece : (o + 1) * self.piece]
         for o, to, place in self.leaves():
-            self.copy(self.t2.at[to], self.r2.at[o], 1, o, place)
+            self.copy(self.t2.at[to], self.r2.at[o], 1, place)
+        self.bulk(1, self.r2.at[1:])
 
     def gather_leaf(self):
         self.arrived()
@@ -166,7 +173,8 @@
         self.r3[self.sib, self.leaf] = total
         mine = self.r3.at[self.sib, self.leaf]
         for o, to, place in self.leaves():
-            self.copy(mine, mine, 2, o, place)
+            self.copy(mine, mine, 2, place)
+        self.bulk(2, self.r3.at[0, 1:])
 
     def gather_sib(self):
         self.arrived()
@@ -177,7 +185,8 @@
             self.r3[self.sib, 0] = total
         mine = self.r3.at[self.sib]
         for o, to, place in self.sibs():
-            self.copy(mine, mine, 3, o, place)
+            self.copy(mine, mine, 3, place)
+        self.bulk(3, self.r3.at[1:])
 
     def result(self):
         while self.steps:
@@ -212,8 +221,8 @@
     windows, scratch = scratch[: 2 * ITERS], scratch[2 * ITERS :]
     h_send, h_recv, lifted, lifted_t, powers, x_first, work, d_high, d_low = scratch[:9]
     scratch = scratch[9:]
-    sums = [Sum((leaf, sib), sizes, scratch[13 * i : 13 * i + 13]) for i in range(len(COUNTS))]
-    moment_sums, image_sums = sums[1:3], sums[3:]
+    sums = [Sum((leaf, sib), sizes, scratch[7 * i : 7 * i + 7]) for i in range(len(COUNTS))]
+    moment_sum, early, late = sums[1:]
 
     def place(p):
         return (p // n_sib, lax.rem(p, n_sib))
@@ -338,10 +347,9 @@
             powers[j, rows, :] = value
             if j + 1 < ITERS:
                 send_block(j + 1, i, value)
-        part = j % 2
-        moment_sums[j // 2].src[part * rank : (part + 1) * rank, :] = project(image)
-        if part:
-            moment_sums[j // 2].step()
+        moment_sum.src[j * rank : (j + 1) * rank, :] = project(image)
+        if j + 1 == ITERS:
+            moment_sum.step()
 
     sums[0].step()
     sums[0].step()
@@ -374,13 +382,14 @@
             now.append(x_first[rows, :] - inverse_times(i, image[i]))
             if k + 1 < ITERS:
                 send_block(base + k + 1, i, now[i])
-        image_sums[k].src[...] = project(image)
-        image_sums[k].step()
-        moment_sums[0].step()
-        for j in range(k):
-            image_sums[j].step()
+        target = early if k < 2 else late
+        target.src[(k % 2) * rank : (k % 2 + 1) * rank, :] = project(image)
+        if k == 3:
+            late.step()
+        if k >= 1:
+            early.step()
         if k >= 2:
-            moment_sums[1].step()
+            moment_sum.step()
         if k + 2 < ITERS:
             power(k + 2)
         if k + 1 < ITERS:
@@ -389,41 +398,45 @@
 
     inverse = work[...]
     deltas = [mm(inverse, first) - start]
-    moments = moment_sums[0].result()
-    moment = [moments[:rank], moments[rank:]]
-
-    def known(k):
-        return sum(mm(moment[j], deltas[k - 1 - j]) for j in range(k))
+    spread = [mm(lifted[rows, :], inverse) for rows in blocks]
+    shift = [mm(powers[0, rows, :], inverse) for rows in blocks]
+    late.step()
+    early.step()
+    moment_sum.step()
+    images = early.result()
+    late.step()
+    moments = moment_sum.result()
+    moment = [moments[j * rank : (j + 1) * rank] for j in range(ITERS)]
 
     def solve(k):
-        deltas.append(deltas[0] + mm(inverse, known(k) - image_sums[k - 1].result()))
-
+        total = sum(mm(moment[j], deltas[k - 1 - j]) for j in range(k))
+        if k <= 2:
+            total -= images[(k - 1) * rank : k * rank]
+        deltas.append(deltas[0] + mm(inverse, total))
+
+    again = mm(moment[0], inverse)
     solve(1)
-    image_sums[-1].step()
-    for s in (moment_sums[1], *image_sums[1:-1]):
-        s.step()
     solve(2)
-    image_sums[-1].step()
-    moments = moment_sums[1].result()
-    moment += [moments[:rank], moments[rank:]]
+    late.step()
     solve(3)
-
-    part = deltas[0] + mm(inverse, known(ITERS))
-    deltas.append(part)
+    solve(4)
     for i, rows in enumerate(blocks):
-        value = now[i] - mm(lifted[rows, :], part)
+        value = now[i] - mm(lifted[rows, :], deltas[ITERS])
         for j in range(1, ITERS + 1):
             value -= mm(powers[j - 1, rows, :], deltas[ITERS - j])
         sol[rows, :] = value
-        lifted[rows, :] = mm(lifted[rows, :], inverse)
-    final = image_sums[-1].result()
+        x_first[rows, :] = shift[i] + mm(spread[i], again)
+        lifted[rows, :] = spread[i]
+    coef[...] = start + deltas[ITERS]
+    twice = mm(inverse, again)
+    final = late.result()
+    before, final = final[:rank], final[rank:]
     for rows in blocks:
-        sol[rows, :] += mm(lifted[rows, :], final)
-    coef[...] = start + part - mm(inverse, final)
+        sol[rows, :] += mm(x_first[rows, :], before) + mm(lifted[rows, :], final)
+    coef[...] -= mm(twice, before) + mm(inverse, final)
 
     for s in sums:
-        for c in s.open:
-            c.wait_send()
+        s.sent()
     for k in range(2 * ITERS):
         for i in range(leaf_dev):
             up, down = halo(k, i)
@@ -462,10 +475,10 @@
         pltpu.VMEM(diagonal_inverse.shape, jnp.bfloat16),
         pltpu.VMEM(diagonal_inverse.shape, jnp.bfloat16),
     ]
-    for n, count in enumerate(COUNTS):
+    for count in COUNTS:
         total = count * rank
         chunk = total // n_sib
-        cut = parted(total, (n_leaf, n_sib), n + 1 == len(COUNTS))
+        cut = parted(total, (n_leaf, n_sib))
         parts = n_leaf if cut else 1
         piece = chunk // parts
         scratch += [
@@ -475,8 +488,7 @@
             pltpu.VMEM((n_leaf, piece, columns), f32),
             pltpu.VMEM((n_sib, parts, piece, columns), f32),
         ]
-        for n in (n_sib, n_leaf, n_leaf, n_sib):
-            scratch += [pltpu.SemaphoreType.DMA((n,)), pltpu.SemaphoreType.DMA((n,))]
+        scratch += [pltpu.SemaphoreType.DMA((4,)), pltpu.SemaphoreType.DMA((4,))]
     vmem = pl.BlockSpec(memory_space=pltpu.VMEM)
     return pl.pallas_call(
         functools.partial(kernel, (n_leaf, n_sib)),

time: 75.2 us -> 71.6 us (0.952)
  Pallas kernels: 71.2 us -> 67.6 us
    pallas_call x1, Pallas kernels: 71.2 us -> 67.6 us  [on_device(): pl.pallas_call(functools.partial(kernel, (n_leaf, n_sib)), out_shape=(jax...]
where the time goes in v4:
time: 71.6 us; the launch traced here: 71.4 us
  Pallas kernels  67.6 us (94%)
  local copies, waits for them, and re-layouts  3.14 us (4%)
    pallas_call x1, Pallas kernels, on_device(): pl.pallas_call(functools.partial(kernel, (n_leaf, n_sib)), out_shape=(jax...  67.6 us
    unnamed x2, local copies, waits for them, and re-layouts  3.14 us

profile of v4, /device:TPU:0, one launch (start us, length us, event | category | flops | bytes accessed | tf_op | source)
XLA Modules:
  0.0 71.4 jit_solution(3249255901689760492)
XLA Ops:
  0.6 67.6 %shard_map.77 = (f32[512,128]{1,0:T(8,128)}, f32[128,128]{1,0:T(8,128)}) custom-call(s32[2,8]{1,0:T(2,128)} %near_in.1, s32[2,1,256]{2,1,0:T(1,128)} %bitcast.1, f32[512,128]{1,0:T(8,128)} %src_in.1, f32[2,256,256]{2,1,0:T(8,128)} %diag_in.1, f32[512,128]{1,0:T(8,128)} %low_in.1, bf16[2,8,256,256]{3,2,1,0:T(8,128)(2,1)} %nearby_in.1), custom_call_target="tpu_custom_call" | custom-call | tf_op jit(solution)/shard_map/pallas_call | solution.py:493
  68.2 1.7 %copy.10 = f32[512,128]{1,0:T(8,128)} copy(f32[512,128]{1,0:T(8,128)} %get-tuple-element.4) | data formatting | bytes 524288
  69.9 1.5 %copy.11 = f32[128,128]{1,0:T(8,128)} copy(f32[128,128]{1,0:T(8,128)} %get-tuple-element.5) | data formatting | bytes 131072

commit v5 on v4

--- a/solution.py
+++ b/solution.py
@@ -288,7 +288,16 @@
         return total
 
     def project(values):
-        return sum(mm(lifted_t[:, blocks[i]], values[i]) for i in range(leaf_dev))
+        total = 0.0
+        for rows, v in zip(blocks, values):
+            high, rest = split(v)
+            left, left_rest = split(lifted_t[:, rows])
+            wide = jnp.dot(
+                left, jnp.concatenate([high, rest], axis=1), preferred_element_type=jnp.float32
+            )
+            small = jnp.dot(left_rest, high, preferred_element_type=jnp.float32)
+            total += wide[:, :columns] + (wide[:, columns:] + small)
+        return total
 
     def inverse_times(i, v):
         high, rest = split(v)

time: 71.6 us -> 71.5 us (level)
  no operation moved by 1% of the time
where the time goes in v5:
time: 71.5 us; the launch traced here: 71.3 us
  Pallas kernels  67.5 us (94%)
  local copies, waits for them, and re-layouts  3.14 us (4%)
    pallas_call x1, Pallas kernels, on_device(): pl.pallas_call(functools.partial(kernel, (n_leaf, n_sib)), out_shape=(jax...  67.5 us
    unnamed x2, local copies, waits for them, and re-layouts  3.14 us

profile of v5, /device:TPU:0, one launch (start us, length us, event | category | flops | bytes accessed | tf_op | source)
XLA Modules:
  0.0 71.3 jit_solution(2408352381300831243)
XLA Ops:
  0.6 67.5 %shard_map.77 = (f32[512,128]{1,0:T(8,128)}, f32[128,128]{1,0:T(8,128)}) custom-call(s32[2,8]{1,0:T(2,128)} %near_in.1, s32[2,1,256]{2,1,0:T(1,128)} %bitcast.1, f32[512,128]{1,0:T(8,128)} %src_in.1, f32[2,256,256]{2,1,0:T(8,128)} %diag_in.1, f32[512,128]{1,0:T(8,128)} %low_in.1, bf16[2,8,256,256]{3,2,1,0:T(8,128)(2,1)} %nearby_in.1), custom_call_target="tpu_custom_call" | custom-call | tf_op jit(solution)/shard_map/pallas_call | solution.py:502
  68.2 1.7 %copy.10 = f32[512,128]{1,0:T(8,128)} copy(f32[512,128]{1,0:T(8,128)} %get-tuple-element.4) | data formatting | bytes 524288
  69.8 1.5 %copy.11 = f32[128,128]{1,0:T(8,128)} copy(f32[128,128]{1,0:T(8,128)} %get-tuple-element.5) | data formatting | bytes 131072
